TPU v7x, 32 devices: a whole 2x2x4 slice. The times are simulated.
32 devices in a mesh: seq: 4 (over z), pair: 4 (over y, core), dp: 2 (over x).
Axes of the slice: x: 2, y: 2, z: 4, core: 2. Of those that a mesh axis runs over, the one named last changes fastest.
Arguments:
- embed: bfloat16 [2048, 1536], P(('dp', 'seq')), parts along dimension 0, may hold values from -6 to 6
- attn_gain: float32 [1536], replicated, may hold values from 0.5 to 1.5
- w_query: bfloat16 [1536, 1024], P(None, 'pair'), may hold values from -2.5643096 to 2.5643096
- w_key: bfloat16 [1536, 128], replicated, may hold values from -0.104613624 to 0.104613624
- w_value: bfloat16 [1536, 128], replicated, may hold values from -0.15625 to 0.15625
- w_out: bfloat16 [1024, 1536], P('pair'), may hold values from -0.1875 to 0.1875
- pair_map: bfloat16 [128, 64, 128], P(('dp', 'seq'), 'pair'), parts along dimension 0, may hold values from -6 to 6
- w_row: bfloat16 [1536, 128], replicated, may hold values from -0.625 to 0.625
- w_col: bfloat16 [1536, 128], replicated, may hold values from -0.625 to 0.625
- pair_gain: float32 [128], replicated, may hold values from 0.5 to 1.5
- conv_weight: bfloat16 [3, 3, 128, 128], replicated, may hold values from -0.1875 to 0.1875
Outputs:
- block_out: bfloat16 [2048, 1536], P(('dp', 'seq'), 'pair'), parts along dimension 0
- new_pair: bfloat16 [128, 64, 128], P(('dp', 'seq'), 'pair'), parts along dimension 0
There are 2 independent parts, one for each index of `dp`. A program takes and returns all parts, laid end to end along the dimension named above; an argument that names none is the same for every part. Nothing has to cross between parts.
All inputs are finite; a program needn't handle non-finite values.
Results may differ from a plain program's by a relative error of at most 0.014.
Values may be sent and summed in bfloat16 or wider, within the bound.
A program may use at most 64 MiB of HBM per device.

v0:
```python
import math
import jax
import jax.numpy as jnp
from jax import lax
from jax.sharding import PartitionSpec as P

POOL = 16


def padded_2(block, sides, width):
    for axis, dim in sides:
        count = lax.axis_size(axis)
        forward = [(i, i + 1) for i in range(count - 1)]
        backward = [(target, source) for source, target in forward]
        low = lax.ppermute(
            lax.slice_in_dim(block, block.shape[dim] - width, None, axis=dim), axis, forward
        )
        high = lax.ppermute(lax.slice_in_dim(block, 0, width, axis=dim), axis, backward)
        block = jnp.concatenate([low, block, high], axis=dim)
    return block


def rms_scale(values, gain):
    return values * lax.rsqrt(jnp.mean(values * values, axis=-1, keepdims=True) + 1e-05) * gain


def rotate(tensor, positions):
    half = tensor.shape[-1] // 2
    freq = 10000.0 ** (-jnp.arange(half, dtype=jnp.float32) / half)
    angles = positions[:, None] * freq[None, :]
    cosine = jnp.cos(angles)[:, None, :]
    sine = jnp.sin(angles)[:, None, :]
    first = tensor[..., :half]
    second = tensor[..., half:]
    return jnp.concatenate(
        [first * cosine - second * sine, first * sine + second * cosine], axis=-1
    )


def per_device(
    embed, attn_gain, w_query, w_key, w_value, w_out, pair_map, w_row, w_col, pair_gain, conv_weight
):
    tokens = embed.shape[0]
    head_size = w_key.shape[1]
    local_heads = w_query.shape[1] // head_size
    normed = rms_scale(embed.astype(jnp.float32), attn_gain).astype(jnp.bfloat16)
    positions = (lax.axis_index("seq") * tokens + jnp.arange(tokens)).astype(jnp.float32)
    query = jnp.dot(normed, w_query, preferred_element_type=jnp.float32).reshape(
        tokens, local_heads, head_size
    )
    query = rotate(query, positions).transpose(1, 0, 2).astype(jnp.bfloat16)
    key = jnp.dot(normed, w_key, preferred_element_type=jnp.float32)[:, None, :]
    key = rotate(key, positions)[:, 0, :].astype(jnp.bfloat16)
    value = jnp.dot(normed, w_value, preferred_element_type=jnp.float32).astype(jnp.bfloat16)
    scale = 1.0 / head_size**0.5

    def attend_block(carry, block):
        running_max, running_sum, running_acc = carry
        key_block, value_block = block
        scores = (
            jnp.einsum("hqd,kd->hqk", query, key_block, preferred_element_type=jnp.float32) * scale
        )
        new_max = jnp.maximum(running_max, jnp.max(scores, axis=-1))
        factor = jnp.exp(running_max - new_max)
        terms = jnp.exp(scores - new_max[..., None])
        new_sum = running_sum * factor + jnp.sum(terms, axis=-1)
        mixed = jnp.einsum(
            "hqk,kd->hqd",
            terms.astype(jnp.bfloat16),
            value_block,
            preferred_element_type=jnp.float32,
        )
        return ((new_max, new_sum, running_acc * factor[..., None] + mixed), None)

    initial = (
        jnp.full((local_heads, tokens), -1e30, jnp.float32),
        jnp.zeros((local_heads, tokens), jnp.float32),
        jnp.zeros((local_heads, tokens, head_size), jnp.float32),
    )
    key_piece = lax.all_gather(key, "seq", axis=0, tiled=True)
    value_piece = lax.all_gather(value, "seq", axis=0, tiled=True)
    length = key_piece.shape[0]
    block = math.gcd(length, 1024)
    key_blocks = key_piece.reshape(length // block, block, head_size)
    value_blocks = value_piece.reshape(length // block, block, head_size)
    result, unused = lax.scan(attend_block, initial, (key_blocks, value_blocks))
    final_max, final_sum, final_acc = result
    attended = (final_acc / final_sum[..., None]).astype(jnp.bfloat16)
    attended = attended.transpose(1, 0, 2).reshape(tokens, local_heads * head_size)
    head_terms = jnp.dot(attended, w_out, preferred_element_type=jnp.float32)
    summed = lax.psum_scatter(
        head_terms.astype(jnp.bfloat16), "pair", scatter_dimension=1, tiled=True
    ).astype(jnp.float32)
    feature_count = summed.shape[1]
    residual = lax.dynamic_slice_in_dim(
        embed, lax.axis_index("pair") * feature_count, feature_count, 1
    )
    block_out = (residual.astype(jnp.float32) + summed).astype(jnp.bfloat16)
    model_width = normed.shape[1]
    pooled = jnp.mean(
        normed.astype(jnp.float32).reshape(tokens // POOL, POOL, model_width), axis=1
    ).astype(jnp.bfloat16)
    row_feat = jnp.dot(pooled, w_row, preferred_element_type=jnp.float32).astype(jnp.bfloat16)
    col_feat = jnp.dot(pooled, w_col, preferred_element_type=jnp.float32).astype(jnp.bfloat16)
    all_cols = lax.all_gather(col_feat, "seq", axis=0, tiled=True)
    column_count = pair_map.shape[1]
    my_cols = lax.dynamic_slice_in_dim(
        all_cols, lax.axis_index("pair") * column_count, column_count, 0
    )
    updated = (
        pair_map.astype(jnp.float32)
        + row_feat.astype(jnp.float32)[:, None, :] * my_cols.astype(jnp.float32)[None, :, :]
    )
    pair_normed = rms_scale(updated, pair_gain).astype(jnp.bfloat16)
    padded = padded_2(pair_normed, (("seq", 0), ("pair", 1)), 1)
    row_count = pair_map.shape[0]
    channel_count = pair_map.shape[2]
    convolved = jnp.zeros((row_count * column_count, channel_count), jnp.float32)
    for offset_row in range(3):
        for offset_col in range(3):
            window = padded[
                offset_row : offset_row + row_count, offset_col : offset_col + column_count, :
            ]
            convolved = convolved + jnp.dot(
                window.reshape(row_count * column_count, channel_count),
                conv_weight[offset_row, offset_col],
                preferred_element_type=jnp.float32,
            )
    new_pair = (updated + convolved.reshape(row_count, column_count, channel_count)).astype(
        jnp.bfloat16
    )
    return (block_out, new_pair)


def solution(mesh):
    placed = (
        P(("dp", "seq"), None),
        P(),
        P(None, "pair"),
        P(),
        P(),
        P("pair", None),
        P(("dp", "seq"), "pair", None),
        P(),
        P(),
        P(),
        P(),
    )
    return jax.shard_map(
        per_device,
        mesh=mesh,
        in_specs=placed,
        out_specs=(P(("dp", "seq"), "pair"), P(("dp", "seq"), "pair", None)),
        check_vma=False,
    )
```

profile of v0, /device:TPU:0, one launch (start us, length us, event | category | flops | bytes accessed | tf_op | source)
XLA Modules:
  0.0 97.6 jit_solution(4122709407723177928)
XLA Ops:
  7.3 1.5 %fusion.2 = f32[256]{0:T(256)S(1)} fusion(bf16[256,1536]{1,0:T(8,128)(2,1)} %param.11), kind=kLoop, calls=%fused_computation.7 | loop fusion | flops 1179392 | bytes 787456 | tf_op jit(solution)/shard_map/reduce_sum | solution.py:24
  8.8 1.7 %convert_reduce_fusion = f32[16,1536]{1,0:T(8,128)S(1)} fusion(f32[1536]{0:T(1024)} %param.12, f32[256]{0:T(256)S(1)} %add_rsqrt_fusion.1, bf16[256,1536]{1,0:T(8,128)(2,1)} %param.11), kind=kLoop, calls=%fused_computation.10 | loop fusion | flops 2334720 | bytes 891904 | tf_op jit(solution)/shard_map/reduce_sum | solution.py:100
  10.5 0.2 convolution_convert_fusion.2
  10.7 14.8 %all_gather.11 = bf16[64,128]{1,0:T(8,128)(2,1)S(1)} all-gather(bf16[16,128]{1,0:T(8,128)(2,1)S(1)} %convolution_convert_fusion.2), channel_id=1, replica_groups=mesh['seq'=4,'pair'=4,'dp'=2] {'seq'}, dimensions={0}, use_global_device_ids=true | all-gather | bytes 20480 | tf_op jit(solution)/shard_map/all_gather | solution.py:105
  25.5 0.2 fusion.9
  25.9 1.3 %collective-permute-start.1 = (bf16[1,16,128]{2,1,0:T(8,128)(2,1)S(1)}, bf16[1,16,128]{2,1,0:T(8,128)(2,1)S(1)}, u32[]{:S(2)}, u32[]{:S(2)}) collective-permute-start(bf16[1,16,128]{2,1,0:T(8,128)(2,1)S(1)} %get-tuple-element.42), channel_id=1, source_target_pairs={{8,0},{16,8},{24,16},{9,1},{17,9},{25,17},{10,2},{18,10},{26,18},{... | collective-permute-start | bytes 12296 | tf_op jit(solution)/shard_map/ppermute | solution.py:18
  27.2 4.5 %collective-permute-start = (bf16[1,16,128]{2,1,0:T(8,128)(2,1)S(1)}, bf16[1,16,128]{2,1,0:T(8,128)(2,1)S(1)}, u32[]{:S(2)}, u32[]{:S(2)}) collective-permute-start(bf16[1,16,128]{2,1,0:T(8,128)(2,1)S(1)} %get-tuple-element.41), channel_id=1, source_target_pairs={{0,8},{8,16},{16,24},{1,9},{9,17},{17,25},{2,10},{10,18},{18,26},{... | collective-permute-start | bytes 12296 | tf_op jit(solution)/shard_map/ppermute | solution.py:15
  31.8 0.5 convolution_bitcast_fusion.1
  32.3 0.5 multiply_cosine_fusion
  32.9 0.3 fusion.23
  33.2 13.8 %all-gather = bf16[1024,1,128]{0,2,1:T(8,128)(2,1)S(1)} all-gather(bf16[256,1,128]{0,2,1:T(8,128)(2,1)S(1)} %pad_maximum_fusion.3), channel_id=2, replica_groups=mesh['seq'=4,'pair'=4,'dp'=2] {'seq'}, dimensions={0}, use_global_device_ids=true | all-gather | bytes 327680 | tf_op jit(solution)/shard_map/all_gather | solution.py:80
  47.0 0.6 fusion.52
  48.0 0.6 multiply_reduce_fusion
  48.6 0.4 copy-done.10
  49.0 0.5 convolution_convert_fusion.1
  49.5 13.8 %all_gather.10 = bf16[1024,128]{0,1:T(8,128)(2,1)S(1)} all-gather(bf16[256,128]{0,1:T(8,128)(2,1)S(1)} %convolution_convert_fusion.1), channel_id=1, replica_groups=mesh['seq'=4,'pair'=4,'dp'=2] {'seq'}, dimensions={0}, use_global_device_ids=true | all-gather | bytes 327680 | tf_op jit(solution)/shard_map/all_gather | solution.py:81
  63.2 0.5 fusion
  63.8 0.6 fusion.7
  64.4 0.4 convolution_convert_fusion
  64.8 1.2 %copy.21 = bf16[256,1536]{0,1:T(8,128)(2,1)} copy(bf16[256,1536]{1,0:T(8,128)(2,1)S(1)} %convolution_convert_fusion) | data formatting | bytes 1572864
  66.1 1.3 %collective-permute-start.2 = (bf16[18,1,128]{2,1,0:T(2,128)(2,1)S(1)}, bf16[18,1,128]{2,1,0:T(2,128)(2,1)S(1)}, u32[]{:S(2)}, u32[]{:S(2)}) collective-permute-start(bf16[18,1,128]{2,1,0:T(2,128)(2,1)S(1)} %get-tuple-element.37), channel_id=1, source_target_pairs={{0,2},{2,4},{4,6},{1,3},{3,5},{5,7},{8,10},{10,12},{12,14},{9,11},... | collective-permute-start | bytes 13832 | tf_op jit(solution)/shard_map/ppermute | solution.py:15
  67.4 1.3 %collective-permute-start.3 = (bf16[18,1,128]{2,1,0:T(2,128)(2,1)S(1)}, bf16[18,1,128]{2,1,0:T(2,128)(2,1)S(1)}, u32[]{:S(2)}, u32[]{:S(2)}) collective-permute-start(bf16[18,1,128]{2,1,0:T(2,128)(2,1)S(1)} %get-tuple-element.38), channel_id=1, source_target_pairs={{2,0},{4,2},{6,4},{3,1},{5,3},{7,5},{10,8},{12,10},{14,12},{11,9},... | collective-permute-start | bytes 13832 | tf_op jit(solution)/shard_map/ppermute | solution.py:18
  68.8 3.3 %collective-permute-done.3 = bf16[18,1,128]{2,1,0:T(2,128)(2,1)S(1)} collective-permute-done((bf16[18,1,128]{2,1,0:T(2,128)(2,1)S(1)}, bf16[18,1,128]{2,1,0:T(2,128)(2,1)S(1)}, u32[]{:S(2)}, u32[]{:S(2)}) %collective-permute-start.3) | collective-permute-done | bytes 4640 | tf_op jit(solution)/shard_map/ppermute | solution.py:18
  72.7 0.1 convolution_add_fusion.4
  72.9 0.1 convolution_add_fusion.3
  73.1 0.1 convolution_add_fusion.2
  73.2 0.1 convolution_add_fusion.1
  73.4 0.1 fusion.8
  73.5 0.7 add_convert_fusion.2
  74.2 14.7 %reduce-scatter.4.cloned.1.call-done = bf16[384,256]{1,0:T(8,128)(2,1)} async-done(((bf16[1536,256]{1,0:T(8,128)(2,1)}), bf16[384,256]{1,0:T(8,128)(2,1)}) %reduce-scatter.4.cloned.1.call-update) | async-done | bytes 196624
  88.9 1.1 %copy.22 = bf16[256,384]{1,0:T(8,128)(2,1)S(1)} copy(bf16[256,384]{0,1:T(8,128)(2,1)} %bitcast.103) | data formatting | bytes 393216
  90.0 0.7 add_convert_fusion
  (49 shorter events, 1.4 us)
Async XLA Ops:
  7.2 57.2 %copy-start = (bf16[256,1536]{1,0:T(8,128)(2,1)S(1)}, bf16[256,1536]{1,0:T(8,128)(2,1)}, u32[]{:S(2)}) copy-start(bf16[256,1536]{1,0:T(8,128)(2,1)} %param.16) | copy-start | bytes 2359300
  7.2 24.6 %copy-start.1 = (bf16[256,1536]{1,0:T(8,128)(2,1)S(1)}, bf16[256,1536]{1,0:T(8,128)(2,1)}, u32[]{:S(2)}) copy-start(bf16[256,1536]{1,0:T(8,128)(2,1)} %param.11) | copy-start | bytes 2359300
  7.2 24.6 %copy-start.6 = (f32[1536]{0:T(1024)S(1)}, f32[1536]{0:T(1024)}, u32[]{:S(2)}) copy-start(f32[1536]{0:T(1024)} %param.12) | copy-start | bytes 18436
  7.2 3.3 %copy-start.4 = (bf16[1536,128]{1,0:T(8,128)(2,1)S(1)}, bf16[1536,128]{1,0:T(8,128)(2,1)}, u32[]{:S(2)}) copy-start(bf16[1536,128]{1,0:T(8,128)(2,1)} %param.19) | copy-start | bytes 1179652
  7.2 18.3 %copy-start.3 = (bf16[1536,128]{1,0:T(8,128)(2,1)S(1)}, bf16[1536,128]{1,0:T(8,128)(2,1)}, u32[]{:S(2)}) copy-start(bf16[1536,128]{1,0:T(8,128)(2,1)} %param.18) | copy-start | bytes 1179652
  7.2 18.4 %copy-start.2 = (bf16[16,16,128]{2,1,0:T(8,128)(2,1)S(1)}, bf16[16,16,128]{2,1,0:T(8,128)(2,1)}, u32[]{:S(2)}) copy-start(bf16[16,16,128]{2,1,0:T(8,128)(2,1)} %param.17) | copy-start | bytes 196612
  7.2 18.6 %copy-start.7 = (f32[128]{0:T(128)S(1)}, f32[128]{0:T(128)}, u32[]{:S(2)}) copy-start(f32[128]{0:T(128)} %param.20) | copy-start | bytes 1540
  7.2 24.6 %copy-start.9 = (bf16[1536,128]{1,0:T(8,128)(2,1)S(1)}, bf16[1536,128]{1,0:T(8,128)(2,1)}, u32[]{:S(2)}) copy-start(bf16[1536,128]{1,0:T(8,128)(2,1)} %param.14) | copy-start | bytes 1179652
  7.3 81.7 %reduce-scatter.4.cloned.1.call-start = ((), (), s32[]{:S(2)}) async-start(), calls=%async_computation.1 | async-start | bytes 983040
  25.5 21.5 %copy-start.8 = (bf16[1536,256]{1,0:T(8,128)(2,1)S(1)}, bf16[1536,256]{1,0:T(8,128)(2,1)}, u32[]{:S(2)}) copy-start(bf16[1536,256]{1,0:T(8,128)(2,1)} %param.13) | copy-start | bytes 2359300
  25.9 40.1 %collective-permute-start.1 = (bf16[1,16,128]{2,1,0:T(8,128)(2,1)S(1)}, bf16[1,16,128]{2,1,0:T(8,128)(2,1)S(1)}, u32[]{:S(2)}, u32[]{:S(2)}) collective-permute-start(bf16[1,16,128]{2,1,0:T(8,128)(2,1)S(1)} %get-tuple-element.42), channel_id=1, source_target_pairs={{8,0},{16,8},{24,16},{9,1},{17,9},{25,17},{10,2},{18,10},{26,18},{... | collective-permute-start | bytes 12296 | tf_op jit(solution)/shard_map/ppermute | solution.py:18
  27.2 38.8 %collective-permute-start = (bf16[1,16,128]{2,1,0:T(8,128)(2,1)S(1)}, bf16[1,16,128]{2,1,0:T(8,128)(2,1)S(1)}, u32[]{:S(2)}, u32[]{:S(2)}) collective-permute-start(bf16[1,16,128]{2,1,0:T(8,128)(2,1)S(1)} %get-tuple-element.41), channel_id=1, source_target_pairs={{0,8},{8,16},{16,24},{1,9},{9,17},{17,25},{2,10},{10,18},{18,26},{... | collective-permute-start | bytes 12296 | tf_op jit(solution)/shard_map/ppermute | solution.py:15
  48.0 1.0 %copy-start.10 = (bf16[1536,128]{1,0:T(8,128)(2,1)S(1)}, bf16[1536,128]{1,0:T(8,128)(2,1)}, u32[]{:S(2)}) copy-start(bf16[1536,128]{1,0:T(8,128)(2,1)} %param.15) | copy-start | bytes 1179652
  64.8 3.9 %copy-start.5 = (bf16[3,3,128,128]{3,2,1,0:T(8,128)(2,1)S(1)}, bf16[3,3,128,128]{3,2,1,0:T(8,128)(2,1)}, u32[]{:S(2)}) copy-start(bf16[3,3,128,128]{3,2,1,0:T(8,128)(2,1)} %param.21) | copy-start | bytes 884740
  66.1 2.8 %collective-permute-start.2 = (bf16[18,1,128]{2,1,0:T(2,128)(2,1)S(1)}, bf16[18,1,128]{2,1,0:T(2,128)(2,1)S(1)}, u32[]{:S(2)}, u32[]{:S(2)}) collective-permute-start(bf16[18,1,128]{2,1,0:T(2,128)(2,1)S(1)} %get-tuple-element.37), channel_id=1, source_target_pairs={{0,2},{2,4},{4,6},{1,3},{3,5},{5,7},{8,10},{10,12},{12,14},{9,11},... | collective-permute-start | bytes 13832 | tf_op jit(solution)/shard_map/ppermute | solution.py:15
  67.4 4.8 %collective-permute-start.3 = (bf16[18,1,128]{2,1,0:T(2,128)(2,1)S(1)}, bf16[18,1,128]{2,1,0:T(2,128)(2,1)S(1)}, u32[]{:S(2)}, u32[]{:S(2)}) collective-permute-start(bf16[18,1,128]{2,1,0:T(2,128)(2,1)S(1)} %get-tuple-element.38), channel_id=1, source_target_pairs={{2,0},{4,2},{6,4},{3,1},{5,3},{7,5},{10,8},{12,10},{14,12},{11,9},... | collective-permute-start | bytes 13832 | tf_op jit(solution)/shard_map/ppermute | solution.py:18
Sparse Core Ops, SparseCore 0:
  66.1 22.7 reduce-scatter.3
where the time goes:
time: 97.9 us; the launch traced here: 97.6 us
  blocking collectives  42.4 us (43%)
  waiting for transfers between devices  18.1 us (18%)
  between operations  14.5 us (15%)
  starting transfers between devices  8.46 us (9%)
  other arithmetic  6.37 us (7%)
  matrix products  4.75 us (5%)
  local copies, waits for them, and re-layouts  3.04 us (3%)
    all_gather x1, blocking collectives, per_device(): all_cols = lax.all_gather(col_feat, 'seq', axis=0, tiled=True)  14.8 us
    unnamed x2, waiting for transfers between devices  14.8 us
    all_gather x1, blocking collectives, per_device(): key_piece = lax.all_gather(key, 'seq', axis=0, tiled=True)  13.8 us
    all_gather x1, blocking collectives, per_device(): value_piece = lax.all_gather(value, 'seq', axis=0, tiled=True)  13.8 us
    ppermute x2, starting transfers between devices, padded_2(): lax.ppermute(lax.slice_in_dim(block, block.shape[dim] - width, None, axis...  5.84 us
    ppermute x2, waiting for transfers between devices, padded_2(): lax.ppermute(lax.slice_in_dim(block, 0, width, axis=dim), axis, backward)  3.34 us
    unnamed x26, local copies, waits for them, and re-layouts  2.96 us
    ppermute x2, starting transfers between devices, padded_2(): lax.ppermute(lax.slice_in_dim(block, 0, width, axis=dim), axis, backward)  2.58 us
  transfers between devices with their start and end apart: 5, of which 2 were waited for; matrix products, arithmetic and copies ran while one was open for 8% of the time, Pallas kernels for 0%

commit v1 on v0

--- a/solution.py
+++ b/solution.py
@@ -77,7 +77,16 @@
         jnp.zeros((local_heads, tokens), jnp.float32),
         jnp.zeros((local_heads, tokens, head_size), jnp.float32),
     )
-    key_piece = lax.all_gather(key, "seq", axis=0, tiled=True)
+    ways = lax.axis_size("seq")
+    up = [(d, (d + 1) % ways) for d in range(ways)]
+    down = [(d, (d - 1) % ways) for d in range(ways)]
+    earlier, later = ([key], [key])
+    for _ in range(ways // 2):
+        earlier.append(lax.ppermute(earlier[-1], "seq", up))
+    for _ in range((ways - 1) // 2):
+        later.append(lax.ppermute(later[-1], "seq", down))
+    line = jnp.concatenate([*earlier[::-1], *later[1:]], axis=0)
+    key_piece = jnp.roll(line, (lax.axis_index("seq") - ways // 2) * key.shape[0], axis=0)
     value_piece = lax.all_gather(value, "seq", axis=0, tiled=True)
     length = key_piece.shape[0]
     block = math.gcd(length, 1024)

time: 97.9 us -> 103 us (1.052)
  blocking collectives: 42.4 us -> 27 us
  waiting for transfers between devices: 18.1 us -> 30.5 us
  starting transfers between devices: 8.46 us -> 13.6 us
  matrix products: 4.75 us -> 8.2 us
    all_gather x1 -> x0, blocking collectives: 13.8 us -> none  [per_device(): key_piece = lax.all_gather(key, 'seq', axis=0, tiled=True)]
    unnamed x2, waiting for transfers between devices: 14.8 us -> 20.9 us
    ppermute x0 -> x3, waiting for transfers between devices: none -> 5.9 us  [the longest x2 5.9 us: per_device(): earlier.append(lax.ppermute(earlier[-1], 'seq', up))]
    ppermute x0 -> x3, starting transfers between devices: none -> 5.11 us  [the longest x2 3.08 us: per_device(): earlier.append(lax.ppermute(earlier[-1], 'seq', up))]
    all_gather x1, blocking collectives: 14.8 us -> 13.1 us  [per_device(): all_cols = lax.all_gather(col_feat, 'seq', axis=0, tiled=True)]
    dot_general x1, matrix products: 0.48 us -> 1.79 us  [per_device(): key = jnp.dot(normed, w_key, preferred_element_type=jnp.float32)[:, None, :]]
    reduce_sum x1, other arithmetic: 1.67 us -> 0.5 us  [per_device(): jnp.mean(normed.astype(jnp.float32).reshape(tokens // POOL, POOL, model_w...]
    dot_general x1, matrix products: 0.58 us -> 1.7 us  [per_device(): jnp.dot(normed, w_query, preferred_element_type=jnp.float32)]
  transfers between devices with their start and end apart: 5 -> 8, of which waited for: 2 -> 3; matrix products, arithmetic and copies ran while one was open for 8% -> 8% of each run, Pallas kernels for 0% -> 0%
where the time goes in v1:
time: 103 us
  waiting for transfers between devices  30.5 us (30%)
  blocking collectives  27 us (26%)
  between operations  14.5 us (14%)
  starting transfers between devices  13.6 us (13%)
  matrix products  8.2 us (8%)
  other arithmetic  5.79 us (6%)
  local copies, waits for them, and re-layouts  3.33 us (3%)
    unnamed x2, waiting for transfers between devices  20.9 us
    all_gather x1, blocking collectives, per_device(): value_piece = lax.all_gather(value, 'seq', axis=0, tiled=True)  13.8 us
    all_gather x1, blocking collectives, per_device(): all_cols = lax.all_gather(col_feat, 'seq', axis=0, tiled=True)  13.1 us
    ppermute x2, waiting for transfers between devices, per_device(): earlier.append(lax.ppermute(earlier[-1], 'seq', up))  5.9 us
    ppermute x2, starting transfers between devices, padded_2(): lax.ppermute(lax.slice_in_dim(block, block.shape[dim] - width, None, axis...  5.84 us
    ppermute x2, waiting for transfers between devices, padded_2(): lax.ppermute(lax.slice_in_dim(block, 0, width, axis=dim), axis, backward)  3.76 us
    ppermute x2, starting transfers between devices, per_device(): earlier.append(lax.ppermute(earlier[-1], 'seq', up))  3.08 us
    unnamed x31, local copies, waits for them, and re-layouts  2.62 us
  transfers between devices with their start and end apart: 8, of which 3 were waited for; matrix products, arithmetic and copies ran while one was open for 8% of the time, Pallas kernels for 0%

profile of v1, /device:TPU:0, one launch (start us, length us, event | category | flops | bytes accessed | tf_op | source)
XLA Modules:
  0.0 102.9 jit_solution(9396155344636524600)
XLA Ops:
  7.3 1.5 %fusion.2 = f32[256]{0:T(256)S(1)} fusion(bf16[256,1536]{1,0:T(8,128)(2,1)} %param.11), kind=kLoop, calls=%fused_computation.7 | loop fusion | flops 1179392 | bytes 787456 | tf_op jit(solution)/shard_map/reduce_sum | solution.py:24
  8.8 1.8 %convolution_bitcast_fusion.1 = f32[256,1,128]{0,2,1:T(8,128)S(1)} fusion(bf16[1536,128]{1,0:T(8,128)(2,1)} %param.14, bf16[256,1536]{1,0:T(8,128)(2,1)} %param.11, f32[1536]{0:T(1024)} %param.12, f32[256]{0:T(256)S(1)} %add_rsqrt_fusion.1), kind=kOutput, calls=%fused_computation.15 | convolution fusion | flops 102236160 | bytes 1317888 | tf_op jit(solution)/shard_map/dot_general | solution.py:52
  10.6 0.3 fusion.24
  10.9 0.6 maximum_bitcast_fusion.2
  11.6 3.0 %collective-permute-start = (bf16[256,128]{0,1:T(8,128)(2,1)}, bf16[256,128]{0,1:T(8,128)(2,1)S(1)}, u32[]{:S(2)}, u32[]{:S(2)}) collective-permute-start(bf16[256,128]{0,1:T(8,128)(2,1)} %maximum_bitcast_fusion.2), channel_id=1, source_target_pairs={{0,8},{8,16},{16,24},{24,0},{1,9},{9,17},{17,25},{25,1},{2,10},{10... | collective-permute-start | bytes 196616 | tf_op jit(solution)/shard_map/ppermute | solution.py:85
  14.6 2.0 %collective-permute-start.2 = (bf16[256,128]{0,1:T(8,128)(2,1)}, bf16[256,128]{0,1:T(8,128)(2,1)S(1)}, u32[]{:S(2)}, u32[]{:S(2)}) collective-permute-start(bf16[256,128]{0,1:T(8,128)(2,1)} %maximum_bitcast_fusion.2), channel_id=1, source_target_pairs={{0,24},{8,0},{16,8},{24,16},{1,25},{9,1},{17,9},{25,17},{2,26},{10... | collective-permute-start | bytes 196616 | tf_op jit(solution)/shard_map/ppermute | solution.py:87
  16.6 0.5 convert_reduce_fusion
  17.1 0.2 convolution_convert_fusion.2
  17.3 13.1 %all_gather.7 = bf16[64,128]{1,0:T(8,128)(2,1)S(1)} all-gather(bf16[16,128]{1,0:T(8,128)(2,1)S(1)} %convolution_convert_fusion.2), channel_id=1, replica_groups=mesh['seq'=4,'pair'=4,'dp'=2] {'seq'}, dimensions={0}, use_global_device_ids=true | all-gather | bytes 20480 | tf_op jit(solution)/shard_map/all_gather | solution.py:114
  30.4 0.2 fusion.9
  30.9 1.3 %collective-permute-start.4 = (bf16[1,16,128]{2,1,0:T(8,128)(2,1)S(1)}, bf16[1,16,128]{2,1,0:T(8,128)(2,1)S(1)}, u32[]{:S(2)}, u32[]{:S(2)}) collective-permute-start(bf16[1,16,128]{2,1,0:T(8,128)(2,1)S(1)} %get-tuple-element.42), channel_id=1, source_target_pairs={{8,0},{16,8},{24,16},{9,1},{17,9},{25,17},{10,2},{18,10},{26,18},{... | collective-permute-start | bytes 12296 | tf_op jit(solution)/shard_map/ppermute | solution.py:18
  32.2 4.5 %collective-permute-start.3 = (bf16[1,16,128]{2,1,0:T(8,128)(2,1)S(1)}, bf16[1,16,128]{2,1,0:T(8,128)(2,1)S(1)}, u32[]{:S(2)}, u32[]{:S(2)}) collective-permute-start(bf16[1,16,128]{2,1,0:T(8,128)(2,1)S(1)} %get-tuple-element.41), channel_id=1, source_target_pairs={{0,8},{8,16},{16,24},{1,9},{9,17},{17,25},{2,10},{10,18},{18,26},{... | collective-permute-start | bytes 12296 | tf_op jit(solution)/shard_map/ppermute | solution.py:15
  36.7 0.5 multiply_cosine_fusion
  37.3 1.7 %fusion.54 = f32[256,256]{0,1:T(8,128)S(1)} fusion(bf16[1536,256]{1,0:T(8,128)(2,1)} %param.13, bf16[256,1536]{1,0:T(8,128)(2,1)S(1)} %copy-done.1, f32[1536]{0:T(1024)S(1)} %copy-done.9, f32[256]{0:T(256)S(1)} %add_rsqrt_fusion.1), kind=kOutput, calls=%fused_computation.106 | convolution fusion | flops 202899456 | bytes 1842176 | tf_op jit(solution)/shard_map/dot_general | solution.py:48
  39.3 1.5 %convolution_convert_fusion.1 = bf16[256,128]{0,1:T(8,128)(2,1)S(1)} fusion(bf16[1536,128]{1,0:T(8,128)(2,1)} %param.15, bf16[256,1536]{1,0:T(8,128)(2,1)S(1)} %copy-done.1, f32[1536]{0:T(1024)S(1)} %copy-done.9, f32[256]{0:T(256)S(1)} %add_rsqrt_fusion.1), kind=kOutput, calls=%fused_computation.24 | convolution fusion | flops 102268928 | bytes 1252352 | tf_op jit(solution)/shard_map/dot_general | solution.py:54
  40.9 13.8 %all_gather.6 = bf16[1024,128]{0,1:T(8,128)(2,1)S(1)} all-gather(bf16[256,128]{0,1:T(8,128)(2,1)S(1)} %convolution_convert_fusion.1), channel_id=1, replica_groups=mesh['seq'=4,'pair'=4,'dp'=2] {'seq'}, dimensions={0}, use_global_device_ids=true | all-gather | bytes 327680 | tf_op jit(solution)/shard_map/all_gather | solution.py:90
  54.8 1.3 %collective-permute-start.5 = (bf16[18,1,128]{2,1,0:T(2,128)(2,1)S(1)}, bf16[18,1,128]{2,1,0:T(2,128)(2,1)S(1)}, u32[]{:S(2)}, u32[]{:S(2)}) collective-permute-start(bf16[18,1,128]{2,1,0:T(2,128)(2,1)S(1)} %get-tuple-element.37), channel_id=1, source_target_pairs={{0,2},{2,4},{4,6},{1,3},{3,5},{5,7},{8,10},{10,12},{12,14},{9,11},... | collective-permute-start | bytes 13832 | tf_op jit(solution)/shard_map/ppermute | solution.py:15
  56.1 1.3 %collective-permute-start.6 = (bf16[18,1,128]{2,1,0:T(2,128)(2,1)S(1)}, bf16[18,1,128]{2,1,0:T(2,128)(2,1)S(1)}, u32[]{:S(2)}, u32[]{:S(2)}) collective-permute-start(bf16[18,1,128]{2,1,0:T(2,128)(2,1)S(1)} %get-tuple-element.38), channel_id=1, source_target_pairs={{2,0},{4,2},{6,4},{3,1},{5,3},{7,5},{10,8},{12,10},{14,12},{11,9},... | collective-permute-start | bytes 13832 | tf_op jit(solution)/shard_map/ppermute | solution.py:18
  57.6 3.8 %collective-permute-done.6 = bf16[18,1,128]{2,1,0:T(2,128)(2,1)S(1)} collective-permute-done((bf16[18,1,128]{2,1,0:T(2,128)(2,1)S(1)}, bf16[18,1,128]{2,1,0:T(2,128)(2,1)S(1)}, u32[]{:S(2)}, u32[]{:S(2)}) %collective-permute-start.6) | collective-permute-done | bytes 4640 | tf_op jit(solution)/shard_map/ppermute | solution.py:18
  61.4 0.7 fusion.57
  62.0 0.1 convolution_add_fusion.6
  62.3 0.1 convolution_add_fusion.5
  62.4 5.9 %collective-permute-done.1 = bf16[256,128]{0,1:T(8,128)(2,1)S(1)} collective-permute-done((bf16[256,128]{0,1:T(8,128)(2,1)S(1)}, bf16[256,128]{0,1:T(8,128)(2,1)S(1)}, u32[]{:S(2)}, u32[]{:S(2)}) %collective-permute-start.1) | collective-permute-done | bytes 65568 | tf_op jit(solution)/shard_map/ppermute | solution.py:85
  68.4 0.6 multiply_reduce_fusion
  69.0 0.5 fusion
  69.6 0.6 fusion.7
  70.2 0.4 convolution_convert_fusion
  70.6 1.2 %copy.21 = bf16[256,1536]{0,1:T(8,128)(2,1)} copy(bf16[256,1536]{1,0:T(8,128)(2,1)S(1)} %convolution_convert_fusion) | data formatting | bytes 1572864
  72.8 0.7 add_convert_fusion.2
  73.4 20.9 %reduce-scatter.4.cloned.1.call-done = bf16[384,256]{1,0:T(8,128)(2,1)} async-done(((bf16[1536,256]{1,0:T(8,128)(2,1)}), bf16[384,256]{1,0:T(8,128)(2,1)}) %reduce-scatter.4.cloned.1.call-update) | async-done | bytes 196624
  94.3 1.1 %copy.22 = bf16[256,384]{1,0:T(8,128)(2,1)S(1)} copy(bf16[256,384]{0,1:T(8,128)(2,1)} %bitcast.107) | data formatting | bytes 393216
  95.4 0.7 add_convert_fusion
  (62 shorter events, 1.9 us)
Async XLA Ops:
  7.2 63.0 %copy-start = (bf16[256,1536]{1,0:T(8,128)(2,1)S(1)}, bf16[256,1536]{1,0:T(8,128)(2,1)}, u32[]{:S(2)}) copy-start(bf16[256,1536]{1,0:T(8,128)(2,1)} %param.16) | copy-start | bytes 2359300
  7.2 9.4 %copy-start.1 = (bf16[256,1536]{1,0:T(8,128)(2,1)S(1)}, bf16[256,1536]{1,0:T(8,128)(2,1)}, u32[]{:S(2)}) copy-start(bf16[256,1536]{1,0:T(8,128)(2,1)} %param.11) | copy-start | bytes 2359300
  7.2 9.4 %copy-start.9 = (f32[1536]{0:T(1024)S(1)}, f32[1536]{0:T(1024)}, u32[]{:S(2)}) copy-start(f32[1536]{0:T(1024)} %param.12) | copy-start | bytes 18436
  7.2 87.1 %reduce-scatter.4.cloned.1.call-start = ((), (), s32[]{:S(2)}) async-start(), calls=%async_computation.1 | async-start | bytes 983040
  8.7 8.4 %copy-start.4 = (bf16[1536,128]{1,0:T(8,128)(2,1)S(1)}, bf16[1536,128]{1,0:T(8,128)(2,1)}, u32[]{:S(2)}) copy-start(bf16[1536,128]{1,0:T(8,128)(2,1)} %param.19) | copy-start | bytes 1179652
  8.8 21.7 %copy-start.3 = (bf16[1536,128]{1,0:T(8,128)(2,1)S(1)}, bf16[1536,128]{1,0:T(8,128)(2,1)}, u32[]{:S(2)}) copy-start(bf16[1536,128]{1,0:T(8,128)(2,1)} %param.18) | copy-start | bytes 1179652
  8.8 21.8 %copy-start.2 = (bf16[16,16,128]{2,1,0:T(8,128)(2,1)S(1)}, bf16[16,16,128]{2,1,0:T(8,128)(2,1)}, u32[]{:S(2)}) copy-start(bf16[16,16,128]{2,1,0:T(8,128)(2,1)} %param.17) | copy-start | bytes 196612
  10.6 20.2 %copy-start.10 = (f32[128]{0:T(128)S(1)}, f32[128]{0:T(128)}, u32[]{:S(2)}) copy-start(f32[128]{0:T(128)} %param.20) | copy-start | bytes 1540
  11.6 50.6 %collective-permute-start = (bf16[256,128]{0,1:T(8,128)(2,1)}, bf16[256,128]{0,1:T(8,128)(2,1)S(1)}, u32[]{:S(2)}, u32[]{:S(2)}) collective-permute-start(bf16[256,128]{0,1:T(8,128)(2,1)} %maximum_bitcast_fusion.2), channel_id=1, source_target_pairs={{0,8},{8,16},{16,24},{24,0},{1,9},{9,17},{17,25},{25,1},{2,10},{10... | collective-permute-start | bytes 196616 | tf_op jit(solution)/shard_map/ppermute | solution.py:85
  14.6 53.8 %collective-permute-start.2 = (bf16[256,128]{0,1:T(8,128)(2,1)}, bf16[256,128]{0,1:T(8,128)(2,1)S(1)}, u32[]{:S(2)}, u32[]{:S(2)}) collective-permute-start(bf16[256,128]{0,1:T(8,128)(2,1)} %maximum_bitcast_fusion.2), channel_id=1, source_target_pairs={{0,24},{8,0},{16,8},{24,16},{1,25},{9,1},{17,9},{25,17},{2,26},{10... | collective-permute-start | bytes 196616 | tf_op jit(solution)/shard_map/ppermute | solution.py:87
  30.9 23.9 %collective-permute-start.4 = (bf16[1,16,128]{2,1,0:T(8,128)(2,1)S(1)}, bf16[1,16,128]{2,1,0:T(8,128)(2,1)S(1)}, u32[]{:S(2)}, u32[]{:S(2)}) collective-permute-start(bf16[1,16,128]{2,1,0:T(8,128)(2,1)S(1)} %get-tuple-element.42), channel_id=1, source_target_pairs={{8,0},{16,8},{24,16},{9,1},{17,9},{25,17},{10,2},{18,10},{26,18},{... | collective-permute-start | bytes 12296 | tf_op jit(solution)/shard_map/ppermute | solution.py:18
  32.2 22.6 %collective-permute-start.3 = (bf16[1,16,128]{2,1,0:T(8,128)(2,1)S(1)}, bf16[1,16,128]{2,1,0:T(8,128)(2,1)S(1)}, u32[]{:S(2)}, u32[]{:S(2)}) collective-permute-start(bf16[1,16,128]{2,1,0:T(8,128)(2,1)S(1)} %get-tuple-element.41), channel_id=1, source_target_pairs={{0,8},{8,16},{16,24},{1,9},{9,17},{17,25},{2,10},{10,18},{18,26},{... | collective-permute-start | bytes 12296 | tf_op jit(solution)/shard_map/ppermute | solution.py:15
  39.3 18.1 %copy-start.5 = (bf16[3,3,128,128]{3,2,1,0:T(8,128)(2,1)S(1)}, bf16[3,3,128,128]{3,2,1,0:T(8,128)(2,1)}, u32[]{:S(2)}) copy-start(bf16[3,3,128,128]{3,2,1,0:T(8,128)(2,1)} %param.21) | copy-start | bytes 884740
  54.8 2.8 %collective-permute-start.5 = (bf16[18,1,128]{2,1,0:T(2,128)(2,1)S(1)}, bf16[18,1,128]{2,1,0:T(2,128)(2,1)S(1)}, u32[]{:S(2)}, u32[]{:S(2)}) collective-permute-start(bf16[18,1,128]{2,1,0:T(2,128)(2,1)S(1)} %get-tuple-element.37), channel_id=1, source_target_pairs={{0,2},{2,4},{4,6},{1,3},{3,5},{5,7},{8,10},{10,12},{12,14},{9,11},... | collective-permute-start | bytes 13832 | tf_op jit(solution)/shard_map/ppermute | solution.py:15
  56.1 5.2 %collective-permute-start.6 = (bf16[18,1,128]{2,1,0:T(2,128)(2,1)S(1)}, bf16[18,1,128]{2,1,0:T(2,128)(2,1)S(1)}, u32[]{:S(2)}, u32[]{:S(2)}) collective-permute-start(bf16[18,1,128]{2,1,0:T(2,128)(2,1)S(1)} %get-tuple-element.38), channel_id=1, source_target_pairs={{2,0},{4,2},{6,4},{3,1},{5,3},{7,5},{10,8},{12,10},{14,12},{11,9},... | collective-permute-start | bytes 13832 | tf_op jit(solution)/shard_map/ppermute | solution.py:18
  62.2 6.1 %collective-permute-start.1 = (bf16[256,128]{0,1:T(8,128)(2,1)S(1)}, bf16[256,128]{0,1:T(8,128)(2,1)S(1)}, u32[]{:S(2)}, u32[]{:S(2)}) collective-permute-start(bf16[256,128]{0,1:T(8,128)(2,1)S(1)} %collective-permute-done), channel_id=1, source_target_pairs={{0,8},{8,16},{16,24},{24,0},{1,9},{9,17},{17,25},{25,1},{2,10},{10... | collective-permute-start | bytes 196616 | tf_op jit(solution)/shard_map/ppermute | solution.py:85
  70.6 1.4 %copy-start.8 = (bf16[16,16,128]{2,1,0:T(8,128)(2,1)S(1)}, bf16[16,16,128]{2,1,0:T(8,128)(2,1)}, u32[]{:S(2)}) copy-start(bf16[16,16,128]{2,1,0:T(8,128)(2,1)} %get-tuple-element.30) | copy-start | bytes 196612
  70.6 1.7 %copy-start.7 = (bf16[16,16,128]{2,1,0:T(8,128)(2,1)S(1)}, bf16[16,16,128]{2,1,0:T(8,128)(2,1)}, u32[]{:S(2)}) copy-start(bf16[16,16,128]{2,1,0:T(8,128)(2,1)} %get-tuple-element.51) | copy-start | bytes 196612
  70.6 1.8 %copy-start.6 = (bf16[16,16,128]{2,1,0:T(8,128)(2,1)S(1)}, bf16[16,16,128]{2,1,0:T(8,128)(2,1)}, u32[]{:S(2)}) copy-start(bf16[16,16,128]{2,1,0:T(8,128)(2,1)} %get-tuple-element.29) | copy-start | bytes 196612
Sparse Core Ops, SparseCore 0:
  71.9 22.2 reduce-scatter.3
